TPU v7x, 256 devices: a whole 4x4x8 slice. The times are simulated.
256 devices in a mesh: grp: 8 (over x_hi, y), mem: 32 (over x_lo, z, core).
Axes of the slice: x: 4 (x_hi: 2, x_lo: 2; x = x_hi * 2 + x_lo), y: 4, z: 8, core: 2. Of those that a mesh axis runs over, the one named last changes fastest.
Arguments:
- images: bfloat16 [32768, 1152], P(('grp', 'mem')), may hold values from -1 to 1
- texts: bfloat16 [32768, 1152], P(('grp', 'mem')), may hold values from -1 to 1
- log_temp: float32 [1], replicated, may hold values from 2.3 to 4.6
- bias: float32 [1], replicated, may hold values from -12 to -5
Outputs:
- image_grad: float32 [32768, 1152], P(('grp', 'mem'))
- text_grad: float32 [32768, 1152], P(('grp', 'mem'))
- loss: float32 [1], replicated
- bias_grad: float32 [1], replicated
All inputs are finite; a program needn't handle non-finite values.
Results may differ from a plain program's by a relative error of at most 0.0038.
Values may be sent and summed in bfloat16 or wider, within the bound.
A program may use at most 128 MiB of HBM per device.

v0:
```python
import jax
import jax.numpy as jnp
from jax import lax
from jax.sharding import PartitionSpec as P

ROUNDS = 4


def shifted(shard, axis, by):
    devices = lax.axis_size(axis)
    return lax.ppermute(shard, axis, [(i, (i + by) % devices) for i in range(devices)])


def normalize(values):
    full = values.astype(jnp.float32)
    inverse = lax.rsqrt(jnp.sum(full * full, axis=-1, keepdims=True) + 1e-06)
    return (full * inverse, inverse)


def per_device(images, texts, log_temp, bias):
    rows = images.shape[0]
    width = images.shape[1]
    x_unit, x_inverse = normalize(images)
    y_unit, y_inverse = normalize(texts)
    x_low = x_unit.astype(jnp.bfloat16)
    y_low = y_unit.astype(jnp.bfloat16)
    temp = jnp.exp(log_temp[0])
    offset = bias[0]
    groups = lax.axis_size("grp")
    members = lax.axis_size("mem")
    group = lax.axis_index("grp")
    member = lax.axis_index("mem")
    image_block = lax.all_gather(x_low, "mem", axis=0, tiled=True)
    image_ids = group * members * rows + jnp.arange(image_block.shape[0], dtype=jnp.int32)
    text_local = member * rows + jnp.arange(rows, dtype=jnp.int32)
    loss_sum = jnp.zeros((), jnp.float32)
    c_sum = jnp.zeros((), jnp.float32)
    image_acc = jnp.zeros((image_block.shape[0], width), jnp.float32)
    travel = y_low
    text_home = jnp.zeros((y_low.shape[0], width), jnp.float32)
    for step in range(ROUNDS):
        source = (group - step + groups) % groups
        if step == 0:
            travel = y_low
        else:
            travel = shifted(y_low, "grp", step)
        logits = (
            temp
            * lax.dot_general(
                image_block, travel, (((1,), (1,)), ((), ())), preferred_element_type=jnp.float32
            )
            + offset
        )
        text_ids = source * members * rows + text_local
        sign = jnp.where(image_ids[:, None] == text_ids[None, :], 1.0, -1.0).astype(jnp.float32)
        per = jax.nn.softplus(-sign * logits)
        weight = -sign * jax.nn.sigmoid(-sign * logits)
        weight_low = weight.astype(jnp.bfloat16)
        text_part = lax.dot_general(
            weight_low, image_block, (((0,), (0,)), ((), ())), preferred_element_type=jnp.float32
        )
        part_loss, part_c, weight_low, text_part = (
            jnp.sum(per),
            jnp.sum(weight),
            weight_low,
            text_part,
        )
        loss_sum = loss_sum + part_loss
        c_sum = c_sum + part_c
        image_acc = image_acc + jnp.dot(weight_low, travel, preferred_element_type=jnp.float32)
        if step == 0:
            text_home = text_part
        else:
            text_home = text_home + shifted(text_part, "grp", -step)
    image_mine = lax.psum_scatter(image_acc, "mem", scatter_dimension=0, tiled=True)
    total_loss, total_c = lax.psum((loss_sum, c_sum), ("grp", "mem"))
    gx_full = temp * image_mine
    gy_full = temp * text_home
    image_grad = (gx_full - x_unit * jnp.sum(x_unit * gx_full, axis=-1, keepdims=True)) * x_inverse
    text_grad = (gy_full - y_unit * jnp.sum(y_unit * gy_full, axis=-1, keepdims=True)) * y_inverse
    count = jnp.float32(rows * members * groups)
    return (image_grad, text_grad, (total_loss / count).reshape(1), (total_c / count).reshape(1))


def solution(mesh):
    placed = (P(("grp", "mem"), None), P(("grp", "mem"), None), P(), P())
    return jax.shard_map(
        per_device,
        mesh=mesh,
        in_specs=placed,
        out_specs=(P(("grp", "mem"), None), P(("grp", "mem"), None), P(), P()),
        check_vma=False,
    )
```

profile of v0, /device:TPU:32, one launch (start us, length us, event | category | flops | bytes accessed | tf_op | source)
XLA Modules:
  0.0 408.6 jit_solution(13290424180692340972)
XLA Ops:
  7.2 0.0 all-gather.2.cloned.1.call-start
  7.2 1.1 fusion.25
  8.3 1.8 fusion.21
  10.1 0.0 all-gather.2.cloned.1.call-update
  10.1 0.0 reduce-scatter.2.cloned.1.call-start
  10.2 1.1 fusion.29
  11.3 1.1 fusion.18
  12.4 3.1 collective-permute-start.2
  15.5 3.1 collective-permute-start.1
  18.6 1.0 collective-permute-start
  20.9 64.8 %all-gather.2.cloned.1.call-done = bf16[4096,1152]{1,0:T(8,128)(2,1)} async-done(((bf16[128,1152]{1,0:T(8,128)(2,1)}), bf16[4096,1152]{1,0:T(8,128)(2,1)}) %all-gather.2.cloned.1.call-update) | async-done | bytes 9437200 | tf_op jit(solution)/shard_map/all_gather | solution.py:33
  85.7 7.4 %fusion.2 = f32[4096,128]{1,0:T(8,128)S(1)} fusion(bf16[4096,1152]{1,0:T(8,128)(2,1)} %all-gather.2.cloned.1.call-done, bf16[128,1152]{1,0:T(8,128)(2,1)S(1)} %fusion.18, f32[]{:T(128)} %bitcast.20, f32[]{:T(128)} %bitcast, s32[128]{0:T(128)S(1)} %get-tuple-element.24, s32[4096]{0:T(1024)S(1)} %iota_add_fusion), kind=kOutput, calls=%fused_computation.12 | convolution fusion | flops 1211105280 | bytes 11846152 | tf_op jit(solution)/shard_map/dot_general | solution.py:49
  93.2 7.9 %fusion.41 = f32[4096,1152]{1,0:T(8,128)} fusion(bf16[128,1152]{1,0:T(8,128)(2,1)S(1)} %fusion.18, f32[4096,128]{1,0:T(8,128)S(1)} %fusion.2, s32[128]{0:T(128)S(1)} %get-tuple-element.24, s32[4096]{0:T(1024)S(1)} %iota_add_fusion), kind=kOutput, calls=%fused_computation.64 | convolution fusion | flops 1212153856 | bytes 21283328 | tf_op jit(solution)/shard_map/dot_general | solution.py:70
  101.1 2.7 fusion.4
  103.8 11.8 %convolution_add_fusion.1 = f32[4096,1152]{1,0:T(8,128)} fusion(f32[4096,1152]{1,0:T(8,128)} %fusion.41, bf16[128,1152]{1,0:T(8,128)(2,1)S(1)} %collective-permute-done, f32[4096,128]{1,0:T(8,128)S(1)} %fusion.4, s32[128]{0:T(128)S(1)} %fusion.45, s32[4096]{0:T(1024)S(1)} %iota_add_fusion), kind=kOutput, calls=%fused_computation.2 | convolution fusion | flops 1216872448 | bytes 40157696 | tf_op jit(solution)/shard_map/dot_general | solution.py:70
  115.7 6.2 %fusion.6 = f32[4096,128]{1,0:T(8,128)S(1)} fusion(bf16[4096,1152]{1,0:T(8,128)(2,1)} %all-gather.2.cloned.1.call-done, bf16[128,1152]{1,0:T(8,128)(2,1)S(1)} %collective-permute-done.1, s32[128]{0:T(128)S(1)} %fusion.44, f32[]{:T(128)} %bitcast.22, f32[]{:T(128)} %bitcast, s32[4096]{0:T(1024)S(1)} %iota_add_fusion), kind=kOutput, calls=%fused_computation.16 | convolution fusion | flops 1211105280 | bytes 11846152 | tf_op jit(solution)/shard_map/dot_general | solution.py:49
  121.9 13.3 %fusion.50 = (f32[]{:T(128)}, f32[]{:T(128)}, f32[]{:T(128)}, f32[]{:T(128)}, f32[]{:T(128)}, /*index=5*/f32[]{:T(128)}, f32[]{:T(128)}, f32[]{:T(128)}, f32[4096,128]{1,0:T(8,128)S(1)}) fusion(s32[128]{0:T(128)S(1)} %get-tuple-element.23, s32[4096]{0:T(1024)S(1)} %iota_add_fusion, f32[4096,128]{1,0:T(8,128)S(1)} %fusion.6, s32[128]{0:T(128)S(1)} %fusion.44, ...), kind=kOutput, calls=%fused_computation.77 | convolution fusion | flops 1240989696 | bytes 18139176 | tf_op jit(solution)/shard_map/dot_general | solution.py:49
  135.2 1.3 copy-done.3
  136.5 7.9 %fusion.32 = f32[4096,1152]{1,0:T(8,128)} fusion(bf16[128,1152]{1,0:T(8,128)(2,1)S(1)} %collective-permute-done.2, f32[4096,128]{1,0:T(8,128)S(1)} %get-tuple-element.22, s32[128]{0:T(128)S(1)} %get-tuple-element.23, s32[4096]{0:T(1024)S(1)} %iota_add_fusion), kind=kOutput, calls=%fused_computation.55 | convolution fusion | flops 1212153856 | bytes 21283328 | tf_op jit(solution)/shard_map/dot_general | solution.py:70
  144.5 20.9 %fusion = f32[4096,1152]{1,0:T(8,128)} fusion(f32[4096,1152]{1,0:T(8,128)} %fusion.32, f32[4096,1152]{1,0:T(8,128)} %convolution_add_fusion.1, bf16[128,1152]{1,0:T(8,128)(2,1)S(1)} %collective-permute-done.1, f32[4096,128]{1,0:T(8,128)} %copy-done.6, s32[128]{0:T(128)S(1)} %fusion.44, s32[4096]{0:T(1024)S(1)} %iota_add_fusion), kind=kOutput, calls=%fused_computation.1 | convolution fusion | flops 1221591040 | bytes 59032064 | tf_op jit(solution)/shard_map/dot_general | solution.py:70
  165.3 0.0 reduce-scatter.2.cloned.1.call-update
  165.4 7.8 %fusion.37 = f32[128,1152]{1,0:T(8,128)} fusion(bf16[4096,1152]{1,0:T(8,128)(2,1)} %all-gather.2.cloned.1.call-done, f32[4096,128]{1,0:T(8,128)S(1)} %fusion.4, s32[128]{0:T(128)S(1)} %fusion.45, s32[4096]{0:T(1024)S(1)} %iota_add_fusion), kind=kOutput, calls=%fused_computation.60 | convolution fusion | flops 1212153856 | bytes 12141056 | tf_op jit(solution)/shard_map/dot_general | solution.py:59
  173.2 12.6 %collective-permute-start.3 = (f32[128,1152]{1,0:T(8,128)}, f32[128,1152]{1,0:T(8,128)S(1)}, u32[]{:S(2)}, u32[]{:S(2)}) collective-permute-start(f32[128,1152]{1,0:T(8,128)} %fusion.37), channel_id=1, source_target_pairs={{0,224},{32,0},{64,32},{96,64},{128,96},{160,128},{192,160},{224,1... | collective-permute-start | bytes 1769480 | tf_op jit(solution)/shard_map/ppermute | solution.py:11
  185.8 7.0 %fusion.34 = f32[128,1152]{1,0:T(8,128)} fusion(bf16[4096,1152]{1,0:T(8,128)(2,1)} %all-gather.2.cloned.1.call-done, f32[4096,128]{1,0:T(8,128)S(1)} %copy-done.7, s32[128]{0:T(128)S(1)} %fusion.44, s32[4096]{0:T(1024)S(1)} %iota_add_fusion), kind=kOutput, calls=%fused_computation.57 | convolution fusion | flops 1212153856 | bytes 12141056 | tf_op jit(solution)/shard_map/dot_general | solution.py:59
  192.8 3.1 fusion.30
  195.8 1.3 collective-permute-start.5
  202.3 184.7 %all-reduce = (f32[]{:T(128)}, f32[]{:T(128)}) all-reduce(f32[]{:T(128)S(6)} %add.247, f32[]{:T(128)S(6)} %add.250), channel_id=1, replica_groups=mesh['grp'=8,'mem'=32] {'grp','mem'}, use_global_device_ids=true, to_apply=%region_9.10 | all-reduce | flops 2 | bytes 16 | tf_op jit(solution)/shard_map/psum | solution.py:76
  388.3 0.0 copy-start
  388.4 6.7 %fusion.26 = (f32[128]{0:T(128)S(1)}, f32[128,1152]{1,0:T(8,128)S(1)}) fusion(bf16[128,1152]{1,0:T(8,128)(2,1)S(1)} %copy-done.5, f32[128]{0:T(128)S(1)} %add_rsqrt_fusion, f32[128,1152]{1,0:T(8,128)} %collective-permute-done.5, f32[128,1152]{1,0:T(8,128)} %collective-permute-done.4, f32[128,1152]{1,0:T(8,128)S(1)} %collective-permute-done.3, ...), kind=kOutput, calls=%fused_computation.49 | convolution fusion | flops 1213333376 | bytes 14206468 | tf_op jit(solution)/shard_map/dot_general | solution.py:59
  395.1 1.0 fusion.28
  396.1 1.3 fusion.22
  397.4 2.1 fusion.24
  (42 shorter events, 0.1 us)
Async XLA Ops:
  7.2 78.5 %all-gather.2.cloned.1.call-start = ((), (), s32[]{:S(2)}) async-start(), calls=%async_computation.1 | async-start | bytes 9732096 | tf_op jit(solution)/shard_map/all_gather | solution.py:33
  10.1 386.0 %reduce-scatter.2.cloned.1.call-start = ((), (), s32[]{:S(2)}) async-start(), calls=%async_computation.2 | async-start | bytes 19464192 | tf_op jit(solution)/shard_map/reduce_scatter | solution.py:75
  12.4 109.5 %collective-permute-start.2 = (bf16[128,1152]{1,0:T(8,128)(2,1)S(1)}, bf16[128,1152]{1,0:T(8,128)(2,1)S(1)}, u32[]{:S(2)}, u32[]{:S(2)}) collective-permute-start(bf16[128,1152]{1,0:T(8,128)(2,1)S(1)} %fusion.18), channel_id=1, source_target_pairs={{0,96},{32,128},{64,160},{96,192},{128,224},{160,0},{192,32},{224,... | collective-permute-start | bytes 884744 | tf_op jit(solution)/shard_map/ppermute | solution.py:11
  15.5 100.2 %collective-permute-start.1 = (bf16[128,1152]{1,0:T(8,128)(2,1)S(1)}, bf16[128,1152]{1,0:T(8,128)(2,1)S(1)}, u32[]{:S(2)}, u32[]{:S(2)}) collective-permute-start(bf16[128,1152]{1,0:T(8,128)(2,1)S(1)} %fusion.18), channel_id=1, source_target_pairs={{0,64},{32,96},{64,128},{96,160},{128,192},{160,224},{192,0},{224,... | collective-permute-start | bytes 884744 | tf_op jit(solution)/shard_map/ppermute | solution.py:11
  18.6 82.5 %collective-permute-start = (bf16[128,1152]{1,0:T(8,128)(2,1)S(1)}, bf16[128,1152]{1,0:T(8,128)(2,1)S(1)}, u32[]{:S(2)}, u32[]{:S(2)}) collective-permute-start(bf16[128,1152]{1,0:T(8,128)(2,1)S(1)} %fusion.18), channel_id=1, source_target_pairs={{0,32},{32,64},{64,96},{96,128},{128,160},{160,192},{192,224},{224... | collective-permute-start | bytes 884744 | tf_op jit(solution)/shard_map/ppermute | solution.py:11
  85.7 15.4 %slice-start = ((s8[9437184]{0:T(1024)(128)(4,1)}), s8[4194304]{0:T(1024)(128)(4,1)S(1)}, s32[]{:S(2)}) async-start(s8[9437184]{0:T(1024)(128)(4,1)} %bitcast.24), calls=%async_computation.3 | async-start | bytes 8388608
  85.7 15.4 %slice-start.1 = ((s8[9437184]{0:T(1024)(128)(4,1)}), s8[4194304]{0:T(1024)(128)(4,1)S(1)}, s32[]{:S(2)}) async-start(s8[9437184]{0:T(1024)(128)(4,1)} %bitcast.24), calls=%async_computation.4 | async-start | bytes 8388608
  93.1 28.8 %copy-start.1 = (f32[4096,128]{1,0:T(8,128)}, f32[4096,128]{1,0:T(8,128)S(1)}, u32[]{:S(2)}) copy-start(f32[4096,128]{1,0:T(8,128)S(1)} %fusion.2) | copy-start | bytes 6291460
  93.2 8.0 %slice-start.2 = ((s8[9437184]{0:T(1024)(128)(4,1)}), s8[1048576]{0:T(1024)(128)(4,1)S(1)}, s32[]{:S(2)}) async-start(s8[9437184]{0:T(1024)(128)(4,1)} %bitcast.24), calls=%async_computation.5 | async-start | bytes 2097152
  121.9 13.3 %copy-start.6 = (f32[4096,128]{1,0:T(8,128)}, f32[4096,128]{1,0:T(8,128)S(1)}, u32[]{:S(2)}) copy-start(f32[4096,128]{1,0:T(8,128)S(1)} %fusion.6) | copy-start | bytes 6291460
  135.2 1.3 copy-start.3
  165.4 20.4 %copy-start.7 = (f32[4096,128]{1,0:T(8,128)S(1)}, f32[4096,128]{1,0:T(8,128)}, u32[]{:S(2)}) copy-start(f32[4096,128]{1,0:T(8,128)} %copy-done.6) | copy-start | bytes 6291460
  165.4 27.4 %slice-start.3 = ((s8[9437184]{0:T(1024)(128)(4,1)}), s8[4194304]{0:T(1024)(128)(4,1)S(1)}, s32[]{:S(2)}) async-start(s8[9437184]{0:T(1024)(128)(4,1)} %bitcast.26), calls=%async_computation.6 | async-start | bytes 8388608
  165.4 27.4 %slice-start.4 = ((s8[9437184]{0:T(1024)(128)(4,1)}), s8[4194304]{0:T(1024)(128)(4,1)S(1)}, s32[]{:S(2)}) async-start(s8[9437184]{0:T(1024)(128)(4,1)} %bitcast.26), calls=%async_computation.7 | async-start | bytes 8388608
  173.2 19.5 %copy-start.4 = (f32[4096,128]{1,0:T(8,128)S(1)}, f32[4096,128]{1,0:T(8,128)}, u32[]{:S(2)}) copy-start(f32[4096,128]{1,0:T(8,128)} %copy-done.3) | copy-start | bytes 6291460
  173.2 19.6 %slice-start.5 = ((s8[9437184]{0:T(1024)(128)(4,1)}), s8[1048576]{0:T(1024)(128)(4,1)S(1)}, s32[]{:S(2)}) async-start(s8[9437184]{0:T(1024)(128)(4,1)} %bitcast.26), calls=%async_computation.8 | async-start | bytes 2097152
  173.2 215.1 %collective-permute-start.3 = (f32[128,1152]{1,0:T(8,128)}, f32[128,1152]{1,0:T(8,128)S(1)}, u32[]{:S(2)}, u32[]{:S(2)}) collective-permute-start(f32[128,1152]{1,0:T(8,128)} %fusion.37), channel_id=1, source_target_pairs={{0,224},{32,0},{64,32},{96,64},{128,96},{160,128},{192,160},{224,1... | collective-permute-start | bytes 1769480 | tf_op jit(solution)/shard_map/ppermute | solution.py:11
  192.7 195.6 %copy-start.2 = (f32[4096,128]{1,0:T(8,128)S(1)}, f32[4096,128]{1,0:T(8,128)}, u32[]{:S(2)}) copy-start(f32[4096,128]{1,0:T(8,128)} %copy-done.1) | copy-start | bytes 6291460
  192.7 195.6 %copy-start.5 = (bf16[128,1152]{1,0:T(8,128)(2,1)S(1)}, bf16[128,1152]{1,0:T(8,128)(2,1)}, u32[]{:S(2)}) copy-start(bf16[128,1152]{1,0:T(8,128)(2,1)} %param.5) | copy-start | bytes 884740
  192.7 195.6 %collective-permute-start.4 = (f32[128,1152]{1,0:T(8,128)}, f32[128,1152]{1,0:T(8,128)}, u32[]{:S(2)}, u32[]{:S(2)}) collective-permute-start(f32[128,1152]{1,0:T(8,128)} %fusion.34), channel_id=1, source_target_pairs={{0,192},{32,224},{64,0},{96,32},{128,64},{160,96},{192,128},{224,1... | collective-permute-start | bytes 1769480 | tf_op jit(solution)/shard_map/ppermute | solution.py:11
  195.8 192.5 %collective-permute-start.5 = (f32[128,1152]{1,0:T(8,128)}, f32[128,1152]{1,0:T(8,128)}, u32[]{:S(2)}, u32[]{:S(2)}) collective-permute-start(f32[128,1152]{1,0:T(8,128)} %fusion.30), channel_id=1, source_target_pairs={{0,160},{32,192},{64,224},{96,0},{128,32},{160,64},{192,96},{224,1... | collective-permute-start | bytes 1769480 | tf_op jit(solution)/shard_map/ppermute | solution.py:11
  388.3 7.9 %copy-start = (bf16[128,1152]{1,0:T(8,128)(2,1)S(1)}, bf16[128,1152]{1,0:T(8,128)(2,1)}, u32[]{:S(2)}) copy-start(bf16[128,1152]{1,0:T(8,128)(2,1)} %param.4) | copy-start | bytes 884740
Sparse Core Ops, SparseCore 0:
  10.4 75.2 all-gather.1
  165.5 152.2 reduce-scatter.1
where the time goes:
time: 411 us; the launch traced here: 409 us
  blocking collectives  185 us (45%)
  matrix products  103 us (25%)
  waiting for transfers between devices  64.8 us (16%)
  between operations  24.4 us (6%)
  starting transfers between devices  21.1 us (5%)
  other arithmetic  9.56 us (2%)
    psum x1, blocking collectives, per_device(): total_loss, total_c = lax.psum((loss_sum, c_sum), ('grp', 'mem'))  185 us
    all_gather x1, waiting for transfers between devices, per_device(): image_block = lax.all_gather(x_low, 'mem', axis=0, tiled=True)  64.8 us
    dot_general x4, matrix products, per_device(): jnp.dot(weight_low, travel, preferred_element_type=jnp.float32)  48.6 us
    dot_general x4, matrix products, per_device(): lax.dot_general(image_block, travel, (((1,), (1,)), ((), ())), preferred_...  29.6 us
    dot_general x4, matrix products, per_device(): lax.dot_general(weight_low, image_block, (((0,), (0,)), ((), ())), prefer...  24.6 us
    ppermute x6, starting transfers between devices, shifted(): lax.ppermute(shard, axis, [(i, (i + by) % devices) for i in range(devices)])  21 us
  transfers between devices with their start and end apart: 8, of which 1 were waited for; matrix products, arithmetic and copies ran while one was open for 16% of the time, Pallas kernels for 0%

commit v1 on v0

v1 whole, which is shorter than its diff:
```python
import functools
import math

import jax
import jax.numpy as jnp
from jax import lax
from jax.experimental import pallas as pl
from jax.experimental.pallas import tpu as pltpu
from jax.sharding import PartitionSpec as P

MESH = pl.DeviceIdType.MESH
F32 = jnp.float32
BF16 = jnp.bfloat16
LOG2E = math.log2(math.e)
LN2 = math.log(2.0)

P_SLOT = {0: 0, 1: 2, 3: 3, 2: 5}
S_SLOT = {0: 1, 1: 4, 3: 6, 2: 7}
T_PLACE = {"R1": (0, 0), "L1": (0, 1), "R2": (1, 0), "L2": (1, 1), "R3": (2, 0), "L3": (2, 1), "R0": (3, 0), "L0": (3, 0), "R4": (3, 1), "L4": (3, 1)}


def unit_of(n):
    b = jnp.where(n < 4, n, jnp.where(n < 12, lax.rem(n, 6), jnp.where(n < 21, jnp.minimum(n - 12, 6), jnp.where(n < 28, n - 21, 7))))
    q = jnp.where(n < 6, 0, jnp.where(n < 12, 1, jnp.where(n < 18, 2, jnp.where(n < 21, n - 18, jnp.where(n < 28, 3, n - 28)))))
    return b, q


def log1p_sum(q):
    series = q * (1.0 - q * (0.5 - q * (1.0 / 3.0 - q * 0.25)))
    return jnp.where(q < 0.0078125, series, jnp.log(1.0 + q))


def kernel(
    images, texts, log_temp, bias,
    image_grad, text_grad, loss_out, bias_out,
    ibuf, tbuf, g_i, g_t, cbuf, ctbuf, shift, sums,
    tw_send, tw_recv, pt_send, pt_recv, dr_send, dr_recv, zl_send, zl_recv, zr_send, zr_recv,
    l1, l2, l3, l4, ssem, rsem,
):
    N, W = images.shape
    H = N // 2
    g = lax.axis_index("grp")
    m = lax.axis_index("mem")
    y = lax.rem(g, 4)
    xh = lax.div(g, 4)
    xl = lax.div(m, 16)
    z = lax.rem(lax.div(m, 2), 8)
    core = lax.rem(m, 2)

    def dev(grp, x_lo, zz, cc):
        return (grp, x_lo * 16 + zz * 2 + cc)

    twin = dev(g, xl, z, 1 - core)
    ring = [dev(g, xl, lax.rem(z + k, 8), core) for k in range(8)]
    ahead, back = ring[1], ring[7]
    partner = dev(g, 1 - xl, z, core)
    other = lax.rem(g + 4, 8)
    adjacent = dev(other, 1 - xl, z, core)
    far = dev(other, xl, z, core)
    dest, source = {}, {}
    for r in (1, 2, 3):
        dest[r] = dev(lax.rem(g + r + 4, 8), jnp.where(y + r < 4, 1 - xl, xl), z, core)
        source[r] = dev(lax.rem(g + 12 - r, 8), jnp.where(y - r >= 0, 1 - xl, xl), z, core)

    count = [0]
    started = []

    def message(src, dst, device):
        i = count[0]
        count[0] += 1
        return pltpu.make_async_remote_copy(
            src_ref=src, dst_ref=dst, send_sem=ssem.at[i], recv_sem=rsem.at[i], device_id=device, device_id_type=MESH
        )

    def start(*copies):
        for c in copies:
            c.start()
            started.append(c)

    def place(name, half):
        q, side = T_PLACE[name]
        return tbuf.at[q, pl.ds(side * N + half * H, H)]

    right, left = [], []
    for k in range(7):
        a, b_ = k // 2, k // 2 + 1
        right.append(message(place(f"R{a}", k % 2), place(f"R{b_}", k % 2), ahead))
        left.append(message(place(f"L{a}", 1 - k % 2), place(f"L{b_}", 1 - k % 2), back))

    def own(b):
        return ibuf.at[b, pl.ds(0, N)]

    direct = {r: message(own(0), own(P_SLOT[r]), dest[r]) for r in (1, 3, 2)}
    across = {r: message(own(P_SLOT[r]), own(S_SLOT[r]), partner) for r in (0, 1, 3, 2)}
    twins = [message(own(b), ibuf.at[b, pl.ds(N, N)], twin) for b in range(8)]
    back_twin = [message(tw_send.at[b], tw_recv.at[b], twin) for b in range(8)]
    back_across = {r: message(pt_send.at[r], pt_recv.at[r], partner) for r in range(4)}
    back_direct = {r: message(dr_send.at[r - 1], dr_recv.at[r - 1], source[r]) for r in (1, 2, 3)}
    back_left = [message(zl_send.at[k], zl_recv.at[k], back) for k in range(7)]
    back_right = [message(zr_send.at[k], zr_recv.at[k], ahead) for k in range(7)]
    x = xh * 2 + xl
    loss_twin = message(l1.at[0], l1.at[1], twin)
    loss_ring = [message(l2.at[z], l2.at[z], ring[k]) for k in range(1, 8)]
    loss_row = [message(l3.at[x], l3.at[x], d) for d in (partner, adjacent, far)]
    loss_col = [message(l4.at[y], l4.at[y], dest[r]) for r in (1, 2, 3)]

    peers = [twin, *ring[1:], partner, adjacent, far, *dest.values(), *source.values()]
    barrier = pltpu.get_barrier_semaphore()
    for p in peers:
        pl.semaphore_signal(barrier, inc=1, device_id=p, device_id_type=MESH)

    def unit_rows(ref):
        full = ref[...].astype(F32)
        inverse = lax.rsqrt(jnp.sum(full * full, axis=-1, keepdims=True) + 1e-06)
        return full * inverse, inverse

    tbuf[3, 0:N] = unit_rows(texts)[0].astype(BF16)
    ibuf[0, 0:N] = unit_rows(images)[0].astype(BF16)
    pl.semaphore_wait(barrier, len(peers))
    start(right[0], left[0], across[0], direct[1], direct[3], direct[2], right[1], left[1], twins[0])

    temp = jnp.max(jnp.exp(jnp.full((8, 128), log_temp[0], F32)))
    offset = bias[0]
    scale = temp * LOG2E
    offset2 = offset * LOG2E
    row = lax.broadcasted_iota(jnp.int32, (2 * N, 2 * N), 0)
    col = lax.broadcasted_iota(jnp.int32, (2 * N, 2 * N), 1)
    shift[0] = jnp.full((2 * N, 2 * N), offset2, F32)
    shift[1] = jnp.where((row == col) & (row < N), -1e30, offset2)
    sums[...] = jnp.zeros_like(sums)

    def clear(i, carry):
        zeros = jnp.zeros((32, W), F32)
        g_i[lax.div(i, 8), pl.ds(pl.multiple_of(lax.rem(i, 8) * 32, 32), 32)] = zeros

        @pl.when(i < 32)
        def _():
            g_t[lax.div(i, 8), pl.ds(pl.multiple_of(lax.rem(i, 8) * 32, 32), 32)] = zeros

        return carry

    lax.fori_loop(0, 64, clear, 0)

    def hop(k):
        right[k].wait_recv()
        left[k].wait_recv()
        if k + 2 < 7:
            start(right[k + 2], left[k + 2])

    def logits(b, q):
        return lax.dot_general(ibuf[b], tbuf[q], (((1,), (1,)), ((), ())), preferred_element_type=F32)

    def weights(dots, masked):
        u = dots * scale + shift[masked]
        e = jnp.exp2(-jnp.abs(u))
        d = 1.0 + e
        inv = pl.reciprocal(d, approx=True)
        inv = inv * (2.0 - d * inv)
        c = jnp.where(u >= 0.0, 1.0, e) * inv
        cb = c.astype(BF16)
        cbuf[...] = cb
        ctbuf[...] = cb.T
        parts = [e[8 * i : 8 * i + 8] for i in range(2 * N // 8)]
        while len(parts) > 1:
            parts = [a + (h + a * h) for a, h in zip(parts[::2], parts[1::2])]
        tail = log1p_sum(parts[0])
        linear = jnp.sum(jnp.maximum(u, 0.0).reshape(2 * N // 8, 8, 2 * N), axis=0)
        csum = jnp.sum(c.reshape(2 * N // 8, 8, 2 * N), axis=0)
        sums[0] += tail + linear * LN2
        sums[1] += csum

    def grads(b, q):
        c, ct = cbuf[...], ctbuf[...]
        for lo in range(0, W, 512):
            hi = min(lo + 512, W)
            g_i[b, :, lo:hi] += jnp.dot(c, tbuf[q, :, lo:hi], preferred_element_type=F32)
            g_t[q, :, lo:hi] += jnp.dot(ct, ibuf[b, :, lo:hi], preferred_element_type=F32)

    def pass_on(r):
        direct[r].wait_recv()
        start(across[r], twins[P_SLOT[r]])

    def pass_twin(r):
        across[r].wait_recv()
        start(twins[S_SLOT[r]])

    hop(0)
    hop(1)
    pass_on(1)
    pass_on(3)
    pass_twin(0)
    for b in (0, 1, 2, 3):
        twins[b].wait_recv()

    def step(n, carry):
        @pl.when(n == 4)
        def _():
            hop(2)
            hop(3)
            pass_on(2)
            pass_twin(1)
            twins[4].wait_recv()
            twins[5].wait_recv()

        @pl.when(n == 8)
        def _():
            hop(4)

        @pl.when(n == 12)
        def _():
            hop(5)

        @pl.when(n == 18)
        def _():
            pass_twin(3)
            twins[6].wait_recv()

        @pl.when(n == 21)
        def _():
            hop(6)

        @pl.when(n == 28)
        def _():
            pass_twin(2)
            twins[7].wait_recv()

        b, q = unit_of(n)
        before_b, before_q = unit_of(n - 1)
        dots = logits(b, q)
        grads(before_b, before_q)
        weights(dots, jnp.where(n == 21, 1, 0))
        return carry

    weights(logits(0, 0), 0)
    lax.fori_loop(1, 32, step, 0)
    grads(7, 3)

    def text_part(name, half):
        q, side = T_PLACE[name]
        return g_t[q, side * N + half * H : side * N + half * H + H]

    def ring_back(k):
        name = 4 - (k + 1) // 2
        for sign, send, recv, out in (("R", zl_send, zl_recv, back_left), ("L", zr_send, zr_recv, back_right)):
            half = (k % 2) if sign == "R" else 1 - (k % 2)
            share = text_part(f"{sign}{name}", half)
            if k >= 2:
                out[k - 2].wait_recv()
                share = share + recv[k - 2].astype(F32)
            send[k] = share.astype(BF16)
            start(out[k])

    ring_back(0)
    ring_back(1)
    order = [4, 6, 7, 1, 2, 3, 5, 0]
    for b in order:
        tw_send[b] = g_i[b, N : 2 * N].astype(BF16)
        start(back_twin[b])

    x_unit, x_inverse = unit_rows(images)
    y_unit, y_inverse = unit_rows(texts)
    x_low = x_unit.astype(BF16).astype(F32)
    y_low = y_unit.astype(BF16).astype(F32)
    positive = temp * jnp.sum(x_low * y_low, axis=-1, keepdims=True) + offset
    e = jnp.exp(-jnp.abs(positive))
    d = 1.0 + e
    own_c = -jnp.where(positive >= 0.0, e, 1.0) / d
    own_loss = jnp.maximum(-positive, 0.0) + log1p_sum(e)
    own_cb = own_c.astype(BF16).astype(F32)

    first = lax.broadcasted_iota(jnp.int32, (8, 128), 0) + lax.broadcasted_iota(jnp.int32, (8, 128), 1) == 0
    l1[0, 0:8] = sums[0, :, 0:128] + sums[0, :, 128:256] + jnp.where(first, jnp.sum(own_loss), 0.0)
    l1[0, 8:16] = sums[1, :, 0:128] + sums[1, :, 128:256] + jnp.where(first, jnp.sum(own_c), 0.0)
    start(loss_twin)

    def send_across(r):
        b = S_SLOT[r]
        back_twin[b].wait_recv()
        pt_send[r] = (g_i[b, 0:N] + tw_recv[b].astype(F32)).astype(BF16)
        start(back_across[r])

    def gather_across(r):
        b = P_SLOT[r]
        back_twin[b].wait_recv()
        back_across[r].wait_recv()
        return g_i[b, 0:N] + tw_recv[b].astype(F32) + pt_recv[r].astype(F32)

    def send_home(r):
        dr_send[r - 1] = gather_across(r).astype(BF16)
        start(back_direct[r])

    for r in (1, 3, 2, 0):
        send_across(r)
    loss_twin.wait_recv()
    l2[z] = l1[0] + l1[1]
    start(*loss_ring)
    ring_back(2)
    ring_back(3)
    send_home(1)
    for c in loss_ring:
        c.wait_recv()
    l3[x] = sum([l2[k] for k in range(1, 8)], l2[0])
    start(*loss_row)
    ring_back(4)
    ring_back(5)
    send_home(3)
    for c in loss_row:
        c.wait_recv()
    l4[y] = sum([l3[k] for k in range(1, 4)], l3[0])
    start(*loss_col)
    ring_back(6)
    send_home(2)
    for c in loss_col:
        c.wait_recv()
    total = sum([l4[k] for k in range(1, 4)], l4[0])
    pairs = N * 256
    loss_out[0] = jnp.sum(total[0:8]) / pairs
    bias_out[0] = jnp.sum(total[8:16]) / pairs

    for k in (5, 6):
        back_left[k].wait_recv()
        back_right[k].wait_recv()
    for half in (0, 1):
        rows = slice(half * H, half * H + H)
        side_l = zl_recv[6 if half == 0 else 5].astype(F32)
        side_r = zr_recv[5 if half == 0 else 6].astype(F32)
        gy = temp * (g_t[3, rows] + side_l + side_r + own_cb[rows] * x_low[rows])
        yu = y_unit[rows]
        text_grad[rows] = (gy - yu * jnp.sum(yu * gy, axis=-1, keepdims=True)) * y_inverse[rows]

    gx = gather_across(0) + own_cb * y_low
    for r in (1, 3, 2):
        back_direct[r].wait_recv()
        gx = gx + dr_recv[r - 1].astype(F32)
    gx = temp * gx
    image_grad[...] = (gx - x_unit * jnp.sum(x_unit * gx, axis=-1, keepdims=True)) * x_inverse

    for c in started:
        c.wait_send()


def per_device(images, texts, log_temp, bias):
    N, W = images.shape
    H = N // 2
    vmem = pl.BlockSpec(memory_space=pltpu.VMEM)
    smem = pl.BlockSpec(memory_space=pltpu.SMEM)
    scratch = [
        pltpu.VMEM((8, 2 * N, W), BF16),
        pltpu.VMEM((4, 2 * N, W), BF16),
        pltpu.VMEM((8, 2 * N, W), F32),
        pltpu.VMEM((4, 2 * N, W), F32),
        pltpu.VMEM((2 * N, 2 * N), BF16),
        pltpu.VMEM((2 * N, 2 * N), BF16),
        pltpu.VMEM((2, 2 * N, 2 * N), F32),
        pltpu.VMEM((2, 8, 2 * N), F32),
        pltpu.VMEM((8, N, W), BF16),
        pltpu.VMEM((8, N, W), BF16),
        pltpu.VMEM((4, N, W), BF16),
        pltpu.VMEM((4, N, W), BF16),
        pltpu.VMEM((3, N, W), BF16),
        pltpu.VMEM((3, N, W), BF16),
        pltpu.VMEM((7, H, W), BF16),
        pltpu.VMEM((7, H, W), BF16),
        pltpu.VMEM((7, H, W), BF16),
        pltpu.VMEM((7, H, W), BF16),
        pltpu.VMEM((2, 16, 128), F32),
        pltpu.VMEM((8, 16, 128), F32),
        pltpu.VMEM((4, 16, 128), F32),
        pltpu.VMEM((4, 16, 128), F32),
        pltpu.SemaphoreType.DMA((80,)),
        pltpu.SemaphoreType.DMA((80,)),
    ]
    return pl.pallas_call(
        kernel,
        out_shape=(
            jax.ShapeDtypeStruct((N, W), F32),
            jax.ShapeDtypeStruct((N, W), F32),
            jax.ShapeDtypeStruct((1,), F32),
            jax.ShapeDtypeStruct((1,), F32),
        ),
        in_specs=[vmem, vmem, smem, smem],
        out_specs=(vmem, vmem, smem, smem),
        scratch_shapes=scratch,
        compiler_params=pltpu.CompilerParams(
            collective_id=0, has_side_effects=True, vmem_limit_bytes=58 * 1024 * 1024
        ),
    )(images, texts, log_temp, bias)


def solution(mesh):
    placed = (P(("grp", "mem"), None), P(("grp", "mem"), None), P(), P())
    return jax.shard_map(
        per_device,
        mesh=mesh,
        in_specs=placed,
        out_specs=(P(("grp", "mem"), None), P(("grp", "mem"), None), P(), P()),
        check_vma=False,
    )
```

time: 411 us -> 114 us (0.28)
  blocking collectives: 185 us -> 0 us
  Pallas kernels: 0 us -> 105 us
  matrix products: 103 us -> 0 us
  waiting for transfers between devices: 64.8 us -> 0 us
  starting transfers between devices: 21.1 us -> 0 us
  between operations: 24.4 us -> 5.43 us
  other arithmetic: 9.56 us -> 0 us
    psum x1 -> x0, blocking collectives: 185 us -> none  [per_device(): total_loss, total_c = lax.psum((loss_sum, c_sum), ('grp', 'mem'))]
    pallas_call x0 -> x1, Pallas kernels: none -> 105 us  [per_device(): pl.pallas_call(kernel, out_shape=(jax.ShapeDtypeStruct((N, W), F32), jax....]
    dot_general x12 -> x0, matrix products: 103 us -> none  [the longest x4 48.6 us: per_device(): jnp.dot(weight_low, travel, preferred_element_type=jnp.float32)]
    all_gather x1 -> x0, waiting for transfers between devices: 64.8 us -> none  [per_device(): image_block = lax.all_gather(x_low, 'mem', axis=0, tiled=True)]
    ppermute x6 -> x0, starting transfers between devices: 21 us -> none  [shifted(): lax.ppermute(shard, axis, [(i, (i + by) % devices) for i in range(devices)])]
  transfers between devices with their start and end apart: 8 -> 0, of which waited for: 1 -> 0; matrix products, arithmetic and copies ran while one was open for 16% -> 0% of each run, Pallas kernels for 0% -> 0%
where the time goes in v1:
time: 114 us; the launch traced here: 113 us
  Pallas kernels  105 us (92%)
  between operations  5.43 us (5%)
  local copies, waits for them, and re-layouts  2.8 us (2%)
    pallas_call x1, Pallas kernels, per_device(): pl.pallas_call(kernel, out_shape=(jax.ShapeDtypeStruct((N, W), F32), jax....  105 us
    unnamed x4, local copies, waits for them, and re-layouts  2.8 us

profile of v1, /device:TPU:32, one launch (start us, length us, event | category | flops | bytes accessed | tf_op | source)
XLA Modules:
  0.0 113.1 jit_solution(16568361838687692503)
XLA Ops:
  1.9 104.8 %shard_map.75 = (f32[128,1152]{1,0:T(8,128)}, f32[128,1152]{1,0:T(8,128)}, f32[1]{0:T(128)}, f32[1]{0:T(128)}) custom-call(bf16[128,1152]{1,0:T(8,128)(2,1)} %images.1, bf16[128,1152]{1,0:T(8,128)(2,1)} %texts.1, f32[1]{0:T(128)S(6)} %copy.12.log_temp, f32[1]{0:T(128)S(6)} %copy.13.bias), custom_call_target="tpu_custom_call" | custom-call | tf_op jit(solution)/shard_map/pallas_call | solution.py:373
  106.8 0.0 copy-start
  106.8 2.0 %copy.14 = f32[128,1152]{1,0:T(8,128)} copy(f32[128,1152]{1,0:T(8,128)} %get-tuple-element.8) | data formatting | bytes 1179648
  108.7 0.0 copy-done
  108.8 0.8 copy.15
Async XLA Ops:
  106.8 2.0 %copy-start = (f32[128,1152]{1,0:T(8,128)S(1)}, f32[128,1152]{1,0:T(8,128)}, u32[]{:S(2)}) copy-start(f32[128,1152]{1,0:T(8,128)} %get-tuple-element.9) | copy-start | bytes 1769476

commit v2 on v1

v2 whole, which is shorter than its diff:
```python
import functools
import math

import jax
import jax.numpy as jnp
from jax import lax
from jax.experimental import pallas as pl
from jax.experimental.pallas import tpu as pltpu
from jax.sharding import PartitionSpec as P

MESH = pl.DeviceIdType.MESH
F32 = jnp.float32
BF16 = jnp.bfloat16
LOG2E = math.log2(math.e)
LN2 = math.log(2.0)
SIDE = 64
SIDE_A = 32
MESSAGES_OUT = 40
MESSAGES = 93
SEND_SEMAPHORES = MESSAGES - MESSAGES_OUT


P_SLOT = {0: 0, 1: 2, 3: 3, 2: 6}
S_SLOT = {0: 1, 1: 4, 3: 5, 2: 7}
T_PLACE = {"R1": (0, 0), "L1": (0, 1), "R2": (1, 0), "L2": (1, 1), "R3": (2, 0), "L3": (2, 1), "R0": (3, 0), "L0": (3, 0), "R4": (3, 1), "L4": (3, 1)}


UNITS = (
    (0, 0), (1, 0), (0, 1), (1, 1), (2, 0), (2, 1), (0, 2), (1, 2),
    (2, 2), (3, 0), (3, 1), (3, 2), (3, 3), (2, 3), (1, 3), (0, 3),
)


def unit_of(n):
    p, q = UNITS[0]
    for k in range(1, len(UNITS)):
        p = jnp.where(n == k, UNITS[k][0], p)
        q = jnp.where(n == k, UNITS[k][1], q)
    return p, q


def log1p_sum(q):
    series = q * (1.0 - q * (0.5 - q * (1.0 / 3.0 - q * 0.25)))
    return jnp.where(q < 0.0078125, series, jnp.log(1.0 + q))


def kernel(
    images, texts, log_temp, bias,
    image_grad, text_grad, loss_out, bias_out,
    ibuf, tbuf, tt, g_i, g_t, cbuf, ctbuf, shift, sums, own_weight,
    tw_send, tw_recv, pt_send, pt_recv, dr_send, dr_recv, xa_send, xa_recv, f_send, f_recv,
    sx_send, sx_recv, xs_send, xs_recv, sf_send, sf_recv,
    zl_send, zl_recv, zr_send, zr_recv,
    l1, l2, l3, l4, ssem, rsem,
):
    N, W = images.shape
    H = N // 2
    A = N - SIDE
    C = A + SIDE_A
    g = lax.axis_index("grp")
    m = lax.axis_index("mem")
    y = lax.rem(g, 4)
    xh = lax.div(g, 4)
    xl = lax.div(m, 16)
    z = lax.rem(lax.div(m, 2), 8)
    core = lax.rem(m, 2)
    x = xh * 2 + xl

    def dev(x_hi, yy, x_lo, zz, cc):
        return (x_hi * 4 + lax.rem(yy, 4), x_lo * 16 + lax.rem(zz, 8) * 2 + cc)

    twin = dev(xh, y, xl, z, 1 - core)
    ring = [dev(xh, y, xl, z + k, core) for k in range(8)]
    ahead, back = ring[1], ring[7]
    partner = dev(xh, y, 1 - xl, z, core)
    adjacent = dev(1 - xh, y, 1 - xl, z, core)
    far = dev(1 - xh, y, xl, z, core)
    north, across_y, south = (dev(xh, y + k, xl, z, core) for k in (1, 2, 3))
    up = dev(jnp.where(y == 3, 1 - xh, xh), y + 1, jnp.where(y == 3, 1 - xl, xl), z, core)
    down = dev(jnp.where(y == 0, 1 - xh, xh), y + 3, jnp.where(y == 0, 1 - xl, xl), z, core)

    count = [0]
    started = []

    def message(src, dst, device):
        i = count[0]
        count[0] += 1
        return pltpu.make_async_remote_copy(
            src_ref=src, dst_ref=dst, send_sem=ssem.at[i if i < MESSAGES_OUT else i - MESSAGES_OUT], recv_sem=rsem.at[i],
            device_id=device, device_id_type=MESH,
        )

    def start(*copies):
        for c in copies:
            c.start()
            started.append(c)

    def start_if(where, *copies):
        for c in copies:
            pl.when(where)(c.start)

    def place(name, half):
        q, at = T_PLACE[name]
        return tbuf.at[q, pl.ds(at * N + half * H, H)]

    right, left = [], []
    for k in range(7):
        a, b_ = k // 2, k // 2 + 1
        right.append(message(place(f"R{a}", k % 2), place(f"R{b_}", k % 2), ahead))
        left.append(message(place(f"L{a}", 1 - k % 2), place(f"L{b_}", 1 - k % 2), back))

    def rows_of(b, lo, hi):
        return ibuf.at[b, pl.ds(lo, hi - lo)]

    def move(src, dst, lo, hi, device):
        return message(rows_of(src, lo, hi), rows_of(dst, lo, hi), device)

    halves = ((0, H), (H, N))
    go_north, go_south = jnp.where(y < 3, 8, 0), jnp.where(y == 0, 8, 0)
    swap = [move(0, 8, lo, hi, adjacent) for lo, hi in halves]
    direct = {1: [move(go_north, P_SLOT[1], lo, hi, north) for lo, hi in halves], 3: [move(go_south, P_SLOT[3], lo, hi, south) for lo, hi in halves]}

    direct2 = [move(P_SLOT[1], P_SLOT[2], 0, H, up), move(P_SLOT[3], P_SLOT[2], H, N, down)]
    across = {0: [move(0, S_SLOT[0], lo, hi, partner) for lo, hi in ((A, N), (0, A))]}
    for r in (1, 3, 2):
        across[r] = [move(P_SLOT[r], S_SLOT[r], 0, A, partner)]
    side_swap = move(S_SLOT[0], 9, A, N, adjacent)
    side = {
        1: move(jnp.where(y < 3, 9, S_SLOT[0]), S_SLOT[1], A, N, north),
        3: move(jnp.where(y == 0, 9, S_SLOT[0]), S_SLOT[3], A, N, south),
    }
    side2 = [move(S_SLOT[1], S_SLOT[2], A, C, up), move(S_SLOT[3], S_SLOT[2], C, N, down)]
    twins = [message(rows_of(b, 0, N), rows_of(b, N, 2 * N), twin) for b in range(8)]

    assert count[0] == MESSAGES_OUT
    back_twin = [message(tw_send.at[b], tw_recv.at[b], twin) for b in range(8)]
    back_across = {
        r: message(pt_send.at[r, pl.ds(0, N if r == 0 else A)], pt_recv.at[r, pl.ds(0, N if r == 0 else A)], partner)
        for r in range(4)
    }
    back_direct = {
        r: [message(dr_send.at[i, pl.ds(lo, H)], dr_recv.at[i, pl.ds(lo, H)], d) for lo in (0, H)]
        for i, r, d in ((0, 1, south), (1, 3, north))
    }
    back_swap = [message(xa_send.at[pl.ds(lo, H)], xa_recv.at[pl.ds(lo, H)], adjacent) for lo in (0, H)]
    back_side = {r: message(sx_send.at[i], sx_recv.at[i], d) for i, r, d in ((0, 1, south), (1, 3, north))}
    back_side_swap = message(xs_send, xs_recv, adjacent)

    back_direct2 = [message(f_send.at[i], f_recv.at[i], d) for i, d in ((0, down), (1, up))]
    back_side2 = [message(sf_send.at[i], sf_recv.at[i], d) for i, d in ((0, down), (1, up))]
    back_left = [message(zl_send.at[k], zl_recv.at[k], back) for k in range(7)]
    back_right = [message(zr_send.at[k], zr_recv.at[k], ahead) for k in range(7)]
    loss_twin = message(l1.at[0], l1.at[1], twin)
    loss_ring = [message(l2.at[z], l2.at[z], ring[k]) for k in range(1, 8)]
    loss_row = [message(l3.at[x], l3.at[x], d) for d in (partner, adjacent, far)]
    loss_col = [message(l4.at[y], l4.at[y], d) for d in (north, across_y, south)]

    far_north, far_south = dev(1 - xh, y + 1, 1 - xl, z, core), dev(1 - xh, y + 3, 1 - xl, z, core)

    peers = [twin, *ring[1:], partner, adjacent, far, north, across_y, south, far_north, far_south]
    barrier = pltpu.get_barrier_semaphore()
    for p in peers:
        pl.semaphore_signal(barrier, inc=1, device_id=p, device_id_type=MESH)

    def unit_rows(ref):
        full = ref[...].astype(F32)
        inverse = lax.rsqrt(jnp.sum(full * full, axis=-1, keepdims=True) + 1e-06)
        return full * inverse, inverse

    tbuf[3, 0:N] = unit_rows(texts)[0].astype(BF16)
    ibuf[0, 0:N] = unit_rows(images)[0].astype(BF16)
    pl.semaphore_wait(barrier, len(peers))
    start(right[0], left[0], swap[0], across[0][0])
    start_if(y > 0, direct[3][0])
    start_if(y == 3, direct[1][0])
    start(right[1], left[1], swap[1], across[0][1])
    start_if(y > 0, direct[3][1])
    start_if(y == 3, direct[1][1])
    start(twins[0])
    started.extend(direct[1] + direct[3] + list(side.values()))

    temp = jnp.max(jnp.exp(jnp.full((8, 128), log_temp[0], F32)))
    offset = bias[0]
    scale = temp * LOG2E
    offset2 = offset * LOG2E
    row = lax.broadcasted_iota(jnp.int32, (4 * N, 2 * N), 0)
    col = lax.broadcasted_iota(jnp.int32, (4 * N, 2 * N), 1)
    shift[0] = jnp.full((4 * N, 2 * N), offset2, F32)
    shift[1] = jnp.where((row == col) & (row < N), -1e30, offset2)

    def clear(i, carry):
        zeros = jnp.zeros((32, W), F32)
        g_i[lax.div(i, 8), pl.ds(pl.multiple_of(lax.rem(i, 8) * 32, 32), 32)] = zeros

        @pl.when(i < 32)
        def _():
            g_t[lax.div(i, 8), pl.ds(pl.multiple_of(lax.rem(i, 8) * 32, 32), 32)] = zeros

        return carry

    lax.fori_loop(0, 64, clear, 0)

    positive = temp * jnp.sum(ibuf[0, 0:N].astype(F32) * tbuf[3, 0:N].astype(F32), axis=-1, keepdims=True) + offset
    e_own = jnp.exp(-jnp.abs(positive))
    own_c = -jnp.where(positive >= 0.0, e_own, 1.0) / (1.0 + e_own)
    own_loss = jnp.maximum(-positive, 0.0) + log1p_sum(e_own)
    own_weight[...] = jnp.broadcast_to(own_c.astype(BF16).astype(F32), (N, 128))
    first = lax.broadcasted_iota(jnp.int32, (8, 2 * N), 0) + lax.broadcasted_iota(jnp.int32, (8, 2 * N), 1) == 0
    sums[0] = jnp.where(first, jnp.sum(own_loss), 0.0)
    sums[1] = jnp.where(first, jnp.sum(own_c), 0.0)
    tt[3, :, 0:N] = tbuf[3, 0:N].T

    def hop(k):
        right[k].wait_recv()
        left[k].wait_recv()
        if k + 2 < 7:
            start(right[k + 2], left[k + 2])

    def logits(p, q):
        return jnp.dot(ibuf[pl.ds(2 * p, 2)].reshape(4 * N, W), tt[q], preferred_element_type=F32)

    def weights(dots, masked):
        u = dots * scale + shift[masked]
        e = jnp.exp2(-jnp.abs(u))
        d = 1.0 + e
        inv = pl.reciprocal(d, approx=True)
        inv = inv * (2.0 - d * inv)
        c = jnp.where(u >= 0.0, 1.0, e) * inv
        cb = c.astype(BF16)
        cbuf[...] = cb
        ctbuf[...] = cb.T
        parts = [e[8 * i : 8 * i + 8] for i in range(4 * N // 8)]
        while len(parts) > 1:
            parts = [a + (h + a * h) for a, h in zip(parts[::2], parts[1::2])]
        tail = log1p_sum(parts[0])
        linear = jnp.sum(jnp.maximum(u, 0.0).reshape(4 * N // 8, 8, 2 * N), axis=0)
        csum = jnp.sum(c.reshape(4 * N // 8, 8, 2 * N), axis=0)
        sums[0] += tail + linear * LN2
        sums[1] += csum

    def grads(p, q):
        c, ct = cbuf[...], ctbuf[...]
        for lo, hi in ((0, W),):
            g_i[pl.ds(2 * p, 2), :, lo:hi] += jnp.dot(c, tbuf[q, :, lo:hi], preferred_element_type=F32).reshape(2, 2 * N, hi - lo)
            g_t[q, :, lo:hi] += jnp.dot(
                ct, ibuf[pl.ds(2 * p, 2), :, lo:hi].reshape(4 * N, hi - lo), preferred_element_type=F32
            )

    def text_part(name, half):
        q, at = T_PLACE[name]
        return g_t[q, at * N + half * H : at * N + half * H + H]

    def ring_back(k):
        name = 4 - (k + 1) // 2
        for sign, send, recv, out in (("R", zl_send, zl_recv, back_left), ("L", zr_send, zr_recv, back_right)):
            half = (k % 2) if sign == "R" else 1 - (k % 2)
            share = text_part(f"{sign}{name}", half)
            if k >= 2:
                out[k - 2].wait_recv()
                share = share + recv[k - 2].astype(F32)
            send[k] = share.astype(BF16)
            start(out[k])

    def shared(b, lo, hi):
        return g_i[b, lo:hi] + tw_recv[b, lo:hi].astype(F32)

    def leave_second():
        back_twin[7].wait_recv()
        sf_send[0, 0:SIDE_A] = shared(7, A, C).astype(BF16)
        sf_send[1, 0 : SIDE - SIDE_A] = shared(7, C, N).astype(BF16)
        start(*back_side2)
        pt_send[2, 0:A] = shared(7, 0, A).astype(BF16)
        start(back_across[2])

    def to_twin(b):
        tw_send[b] = g_i[b, N : 2 * N].astype(BF16)
        start(back_twin[b])

    def swapped(i):
        swap[i].wait_recv()
        start_if(y < 3, direct[1][i])
        start_if(y == 0, direct[3][i])

    def arrived(i):
        for r in (1, 3):
            direct[r][i].wait_recv()
        if i == 0:
            start(across[1][0], across[3][0], direct2[0])
        else:
            start(direct2[1], twins[P_SLOT[1]], twins[P_SLOT[3]])

    swapped(0)
    across[0][0].wait_recv()
    start(side_swap)
    start_if(y > 0, side[3])
    start_if(y == 3, side[1])
    hop(0)
    swapped(1)
    hop(1)
    side_swap.wait_recv()
    start_if(y < 3, side[1])
    start_if(y == 0, side[3])
    across[0][1].wait_recv()
    start(twins[S_SLOT[0]])
    arrived(0)
    tt[0] = tbuf[0].T
    twins[0].wait_recv()
    twins[1].wait_recv()

    def step(n, carry):
        @pl.when(n == 1)
        def _():
            arrived(1)
            hop(2)
            side[1].wait_recv()
            side[3].wait_recv()
            start(*side2)
            twins[2].wait_recv()
            twins[3].wait_recv()

        @pl.when(n == 2)
        def _():
            direct2[0].wait_recv()
            start(across[2][0])
            hop(3)
            across[1][0].wait_recv()
            across[3][0].wait_recv()
            start(twins[S_SLOT[1]], twins[S_SLOT[3]])
            tt[1] = tbuf[1].T

        @pl.when(n == 4)
        def _():
            direct2[1].wait_recv()
            start(twins[P_SLOT[2]])
            hop(4)
            twins[4].wait_recv()
            twins[5].wait_recv()

        @pl.when(n == 6)
        def _():
            side2[0].wait_recv()
            side2[1].wait_recv()
            across[2][0].wait_recv()
            start(twins[S_SLOT[2]])
            hop(5)
            tt[2] = tbuf[2].T

        @pl.when(n == 9)
        def _():
            twins[6].wait_recv()
            twins[7].wait_recv()

        @pl.when(n == 12)
        def _():
            hop(6)
            tt[3, :, N : 2 * N] = tbuf[3, N : 2 * N].T

        @pl.when(n == 13)
        def _():
            for c in started:
                c.wait_send()
            started.clear()
            ring_back(1)

        @pl.when(n == 14)
        def _():
            to_twin(7)
            to_twin(6)

        @pl.when(n == 15)
        def _():
            to_twin(4)
            to_twin(5)

        p, q = unit_of(n)
        before_p, before_q = unit_of(n - 1)
        dots = logits(p, q)
        grads(before_p, before_q)
        weights(dots, jnp.where(n == 15, 1, 0))
        return carry

    weights(logits(0, 0), 0)
    lax.fori_loop(1, 16, step, 0)
    grads(0, 3)

    def home(r, lo, hi):
        crossed = N if r == 0 else A
        if hi <= crossed:
            return shared(P_SLOT[r], lo, hi) + pt_recv[r, lo:hi].astype(F32)
        if lo >= crossed:
            return shared(P_SLOT[r], lo, hi)
        return jnp.concatenate([home(r, lo, crossed), home(r, crossed, hi)], axis=0)

    def keep(where, values):
        return jnp.where(where, values.astype(F32), 0.0)

    ring_back(0)
    for b in (2, 3, 1, 0):
        to_twin(b)
    l1[0, 0:8] = sums[0, :, 0:128] + sums[0, :, 128:256]
    l1[0, 8:16] = sums[1, :, 0:128] + sums[1, :, 128:256]
    start(loss_twin)

    leave_second()
    for r in (1, 3):
        back_twin[S_SLOT[r]].wait_recv()
        pt_send[r, 0:A] = shared(S_SLOT[r], 0, A).astype(BF16)
        start(back_across[r])
    ring_back(2)

    for i, r in ((0, 1), (1, 3)):
        b = S_SLOT[r]
        plain, joined = (slice(C, N), slice(A, C)) if i == 0 else (slice(A, C), slice(C, N))
        sx_send[i, plain.start - A : plain.stop - A] = shared(b, plain.start, plain.stop).astype(BF16)
        back_side2[i].wait_recv()
        sx_send[i, joined.start - A : joined.stop - A] = (shared(b, joined.start, joined.stop) + sf_recv[i].astype(F32)).astype(BF16)
        start(back_side[r])
    back_twin[P_SLOT[2]].wait_recv()
    back_across[2].wait_recv()
    f_send[0] = home(2, 0, H).astype(BF16)
    f_send[1] = home(2, H, N).astype(BF16)
    start(*back_direct2)
    loss_twin.wait_recv()
    l2[z] = l1[0] + l1[1]
    start(*loss_ring)
    ring_back(3)
    for r in (1, 3):
        back_side[r].wait_recv()
    xs_send[...] = (keep(y < 3, sx_recv[0]) + keep(y == 0, sx_recv[1])).astype(BF16)
    start(back_side_swap)

    def send_home(r):
        i = r // 2
        back_twin[P_SLOT[r]].wait_recv()
        back_across[r].wait_recv()
        for k in (1 - i, i):
            lo, hi = halves[k]
            share = home(r, lo, hi)
            if k == i:
                back_direct2[i].wait_recv()
                share = share + f_recv[i].astype(F32)
            dr_send[i, lo:hi] = share.astype(BF16)
            start(back_direct[r][k])

    send_home(1)
    ring_back(4)
    send_home(3)
    for c in loss_ring:
        c.wait_recv()
    l3[x] = sum([l2[k] for k in range(1, 8)], l2[0])
    start(*loss_row)
    back_twin[1].wait_recv()
    back_side_swap.wait_recv()
    pt_send[0, 0:A] = shared(1, 0, A).astype(BF16)
    side_sum = keep(y == 3, sx_recv[0]) + keep(y > 0, sx_recv[1]) + xs_recv[...].astype(F32)
    pt_send[0, A:N] = (shared(1, A, N) + side_sum).astype(BF16)
    start(back_across[0])
    ring_back(5)

    def swap_home(k):
        lo, hi = halves[k]
        back_direct[1][k].wait_recv()

        @pl.when(y == 0)
        def _():
            back_direct[3][k].wait_recv()
            xa_send[lo:hi] = (dr_recv[0, lo:hi].astype(F32) + dr_recv[1, lo:hi].astype(F32)).astype(BF16)

        @pl.when(y > 0)
        def _():
            xa_send[lo:hi] = keep(y < 3, dr_recv[0, lo:hi]).astype(BF16)

        start(back_swap[k])

    swap_home(0)
    ring_back(6)
    swap_home(1)
    for c in loss_row:
        c.wait_recv()
    l4[y] = sum([l3[k] for k in range(1, 4)], l3[0])
    start(*loss_col)
    x_unit, x_inverse = unit_rows(images)
    y_unit, y_inverse = unit_rows(texts)
    own_cb = own_weight[:, 0:1]
    for half in (1, 0):
        rows = slice(half * H, half * H + H)
        back_left[6 - half].wait_recv()
        back_right[5 + half].wait_recv()
        came = zl_recv[6 - half].astype(F32) + zr_recv[5 + half].astype(F32)
        gy = temp * (g_t[3, rows] + came + own_cb[rows] * ibuf[0, rows].astype(F32))
        yu = y_unit[rows]
        text_grad[rows] = (gy - yu * jnp.sum(yu * gy, axis=-1, keepdims=True)) * y_inverse[rows]

    back_twin[0].wait_recv()
    back_across[0].wait_recv()
    for k, (lo, hi) in enumerate(halves):
        back_swap[k].wait_recv()
        pl.when(y > 0)(back_direct[3][k].wait_recv)
        came = keep(y == 3, dr_recv[0, lo:hi]) + keep(y > 0, dr_recv[1, lo:hi]) + xa_recv[lo:hi].astype(F32)
        gx = temp * (home(0, lo, hi) + own_cb[lo:hi] * tbuf[3, lo:hi].astype(F32) + came)
        xu = x_unit[lo:hi]
        image_grad[lo:hi] = (gx - xu * jnp.sum(xu * gx, axis=-1, keepdims=True)) * x_inverse[lo:hi]

    for c in loss_col:
        c.wait_recv()
    total = sum([l4[k] for k in range(1, 4)], l4[0])
    pairs = N * 256
    loss_out[...] = jnp.full((1,), jnp.sum(total[0:8]) / pairs, F32)
    bias_out[...] = jnp.full((1,), jnp.sum(total[8:16]) / pairs, F32)

    for c in started:
        c.wait_send()


def per_device(images, texts, log_temp, bias):
    N, W = images.shape
    H = N // 2
    vmem = pl.BlockSpec(memory_space=pltpu.VMEM)
    smem = pl.BlockSpec(memory_space=pltpu.SMEM)
    scratch = [
        pltpu.VMEM((10, 2 * N, W), BF16),
        pltpu.VMEM((4, 2 * N, W), BF16),
        pltpu.VMEM((4, W, 2 * N), BF16),
        pltpu.VMEM((8, 2 * N, W), F32),
        pltpu.VMEM((4, 2 * N, W), F32),
        pltpu.VMEM((4 * N, 2 * N), BF16),
        pltpu.VMEM((2 * N, 4 * N), BF16),
        pltpu.VMEM((2, 4 * N, 2 * N), F32),
        pltpu.VMEM((2, 8, 2 * N), F32),
        pltpu.VMEM((N, 128), F32),
        *[pltpu.VMEM((8, N, W), BF16)] * 2,
        *[pltpu.VMEM((4, N, W), BF16)] * 2,
        *[pltpu.VMEM((2, N, W), BF16)] * 2,
        *[pltpu.VMEM((N, W), BF16)] * 2,
        *[pltpu.VMEM((2, H, W), BF16)] * 2,
        *[pltpu.VMEM((2, SIDE, W), BF16)] * 2,
        *[pltpu.VMEM((SIDE, W), BF16)] * 2,
        *[pltpu.VMEM((2, SIDE_A, W), BF16)] * 2,
        *[pltpu.VMEM((7, H, W), BF16)] * 4,
        pltpu.VMEM((2, 16, 128), F32),
        pltpu.VMEM((8, 16, 128), F32),
        pltpu.VMEM((4, 16, 128), F32),
        pltpu.VMEM((4, 16, 128), F32),
        pltpu.SemaphoreType.DMA((SEND_SEMAPHORES,)),
        pltpu.SemaphoreType.DMA((MESSAGES,)),
    ]
    return pl.pallas_call(
        kernel,
        out_shape=(
            jax.ShapeDtypeStruct((N, W), F32),
            jax.ShapeDtypeStruct((N, W), F32),
            jax.ShapeDtypeStruct((1,), F32),
            jax.ShapeDtypeStruct((1,), F32),
        ),
        in_specs=[vmem, vmem, smem, smem],
        out_specs=(vmem, vmem, vmem, vmem),
        scratch_shapes=scratch,
        compiler_params=pltpu.CompilerParams(
            collective_id=0, has_side_effects=True, vmem_limit_bytes=46 * 1024 * 1024
        ),
    )(images, texts, log_temp, bias)


def solution(mesh):
    placed = (P(("grp", "mem"), None), P(("grp", "mem"), None), P(), P())
    return jax.shard_map(
        per_device,
        mesh=mesh,
        in_specs=placed,
        out_specs=(P(("grp", "mem"), None), P(("grp", "mem"), None), P(), P()),
        check_vma=False,
    )
```

time: 114 us -> 91.9 us (0.81)
  Pallas kernels: 105 us -> 82.7 us
    pallas_call x1, Pallas kernels: 105 us -> 82.7 us  [per_device(): pl.pallas_call(kernel, out_shape=(jax.ShapeDtypeStruct((N, W), F32), jax....]
    unnamed x4 -> x6, local copies, waits for them, and re-layouts: 2.8 us -> 3.55 us
where the time goes in v2:
time: 91.9 us; the launch traced here: 91.7 us
  Pallas kernels  82.7 us (90%)
  between operations  5.44 us (6%)
  local copies, waits for them, and re-layouts  3.55 us (4%)
    pallas_call x1, Pallas kernels, per_device(): pl.pallas_call(kernel, out_shape=(jax.ShapeDtypeStruct((N, W), F32), jax....  82.7 us
    unnamed x6, local copies, waits for them, and re-layouts  3.55 us

profile of v2, /device:TPU:32, one launch (start us, length us, event | category | flops | bytes accessed | tf_op | source)
XLA Modules:
  0.0 91.7 jit_solution(12201150936196580207)
XLA Ops:
  1.9 0.0 copy-start
  1.9 1.0 %copy-done = bf16[128,1152]{1,0:T(8,128)(2,1)S(1)} copy-done((bf16[128,1152]{1,0:T(8,128)(2,1)S(1)}, bf16[128,1152]{1,0:T(8,128)(2,1)}, u32[]{:S(2)}) %copy-start) | copy-done | bytes 294936
  2.9 0.0 copy-start.1
  2.9 1.0 %copy-done.1 = bf16[128,1152]{1,0:T(8,128)(2,1)S(1)} copy-done((bf16[128,1152]{1,0:T(8,128)(2,1)S(1)}, bf16[128,1152]{1,0:T(8,128)(2,1)}, u32[]{:S(2)}) %copy-start.1) | copy-done | bytes 294936
  3.8 82.7 %shard_map.75 = (f32[128,1152]{1,0:T(8,128)S(1)}, f32[128,1152]{1,0:T(8,128)S(1)}, f32[1]{0:T(128)}, f32[1]{0:T(128)}) custom-call(bf16[128,1152]{1,0:T(8,128)(2,1)S(1)} %copy-done, bf16[128,1152]{1,0:T(8,128)(2,1)S(1)} %copy-done.1, f32[1]{0:T(128)S(6)} %copy.12.log_temp, f32[1]{0:T(128)S(6)} %copy.13.bias), custom_call_target="tpu_custom_call" | custom-call | tf_op jit(solution)/shard_map/pallas_call | solution.py:547
  86.5 0.8 copy.14
  87.4 0.8 copy.15
Async XLA Ops:
  1.9 1.0 %copy-start = (bf16[128,1152]{1,0:T(8,128)(2,1)S(1)}, bf16[128,1152]{1,0:T(8,128)(2,1)}, u32[]{:S(2)}) copy-start(bf16[128,1152]{1,0:T(8,128)(2,1)} %images.1) | copy-start | bytes 884740
  2.9 1.0 %copy-start.1 = (bf16[128,1152]{1,0:T(8,128)(2,1)S(1)}, bf16[128,1152]{1,0:T(8,128)(2,1)}, u32[]{:S(2)}) copy-start(bf16[128,1152]{1,0:T(8,128)(2,1)} %texts.1) | copy-start | bytes 884740

commit v3 on v2

--- a/solution.py
+++ b/solution.py
@@ -16,7 +16,7 @@
 SIDE = 64
 SIDE_A = 32
 MESSAGES_OUT = 40
-MESSAGES = 93
+MESSAGES = 94
 SEND_SEMAPHORES = MESSAGES - MESSAGES_OUT
 
 
@@ -134,10 +134,8 @@
 
     assert count[0] == MESSAGES_OUT
     back_twin = [message(tw_send.at[b], tw_recv.at[b], twin) for b in range(8)]
-    back_across = {
-        r: message(pt_send.at[r, pl.ds(0, N if r == 0 else A)], pt_recv.at[r, pl.ds(0, N if r == 0 else A)], partner)
-        for r in range(4)
-    }
+    back_across = {r: message(pt_send.at[r, pl.ds(0, A)], pt_recv.at[r, pl.ds(0, A)], partner) for r in range(4)}
+    back_across_rest = message(pt_send.at[0, pl.ds(A, SIDE)], pt_recv.at[0, pl.ds(A, SIDE)], partner)
     back_direct = {
         r: [message(dr_send.at[i, pl.ds(lo, H)], dr_recv.at[i, pl.ds(lo, H)], d) for lo in (0, H)]
         for i, r, d in ((0, 1, south), (1, 3, north))
@@ -310,40 +308,46 @@
     def step(n, carry):
         @pl.when(n == 1)
         def _():
+            hop(2)
             arrived(1)
-            hop(2)
             side[1].wait_recv()
             side[3].wait_recv()
             start(*side2)
+            hop(3)
+            direct2[0].wait_recv()
+            start(across[2][0])
             twins[2].wait_recv()
             twins[3].wait_recv()
 
         @pl.when(n == 2)
         def _():
-            direct2[0].wait_recv()
-            start(across[2][0])
-            hop(3)
             across[1][0].wait_recv()
             across[3][0].wait_recv()
             start(twins[S_SLOT[1]], twins[S_SLOT[3]])
             tt[1] = tbuf[1].T
 
+        @pl.when(n == 3)
+        def _():
+            hop(4)
+
         @pl.when(n == 4)
         def _():
             direct2[1].wait_recv()
             start(twins[P_SLOT[2]])
-            hop(4)
             twins[4].wait_recv()
             twins[5].wait_recv()
 
         @pl.when(n == 6)
+        def _():
+            hop(5)
+            tt[2] = tbuf[2].T
+
+        @pl.when(n == 7)
         def _():
             side2[0].wait_recv()
             side2[1].wait_recv()
             across[2][0].wait_recv()
             start(twins[S_SLOT[2]])
-            hop(5)
-            tt[2] = tbuf[2].T
 
         @pl.when(n == 9)
         def _():
@@ -400,9 +404,10 @@
     l1[0, 0:8] = sums[0, :, 0:128] + sums[0, :, 128:256]
     l1[0, 8:16] = sums[1, :, 0:128] + sums[1, :, 128:256]
     start(loss_twin)
+    ring_back(3)
 
     leave_second()
-    for r in (1, 3):
+    for r in (1, 3, 0):
         back_twin[S_SLOT[r]].wait_recv()
         pt_send[r, 0:A] = shared(S_SLOT[r], 0, A).astype(BF16)
         start(back_across[r])
@@ -423,7 +428,7 @@
     loss_twin.wait_recv()
     l2[z] = l1[0] + l1[1]
     start(*loss_ring)
-    ring_back(3)
+    ring_back(5)
     for r in (1, 3):
         back_side[r].wait_recv()
     xs_send[...] = (keep(y < 3, sx_recv[0]) + keep(y == 0, sx_recv[1])).astype(BF16)
@@ -442,20 +447,17 @@
             dr_send[i, lo:hi] = share.astype(BF16)
             start(back_direct[r][k])
 
+    ring_back(4)
     send_home(1)
-    ring_back(4)
     send_home(3)
+    back_side_swap.wait_recv()
+    side_sum = keep(y == 3, sx_recv[0]) + keep(y > 0, sx_recv[1]) + xs_recv[...].astype(F32)
+    pt_send[0, A:N] = (shared(1, A, N) + side_sum).astype(BF16)
+    start(back_across_rest)
     for c in loss_ring:
         c.wait_recv()
     l3[x] = sum([l2[k] for k in range(1, 8)], l2[0])
     start(*loss_row)
-    back_twin[1].wait_recv()
-    back_side_swap.wait_recv()
-    pt_send[0, 0:A] = shared(1, 0, A).astype(BF16)
-    side_sum = keep(y == 3, sx_recv[0]) + keep(y > 0, sx_recv[1]) + xs_recv[...].astype(F32)
-    pt_send[0, A:N] = (shared(1, A, N) + side_sum).astype(BF16)
-    start(back_across[0])
-    ring_back(5)
 
     def swap_home(k):
         lo, hi = halves[k]
@@ -472,9 +474,9 @@
 
         start(back_swap[k])
 
+    swap_home(1)
+    ring_back(6)
     swap_home(0)
-    ring_back(6)
-    swap_home(1)
     for c in loss_row:
         c.wait_recv()
     l4[y] = sum([l3[k] for k in range(1, 4)], l3[0])
@@ -493,6 +495,7 @@
 
     back_twin[0].wait_recv()
     back_across[0].wait_recv()
+    back_across_rest.wait_recv()
     for k, (lo, hi) in enumerate(halves):
         back_swap[k].wait_recv()
         pl.when(y > 0)(back_direct[3][k].wait_recv)

time: 91.9 us -> 91.6 us (level); the launches traced: 91.7 us -> 90.4 us
  Pallas kernels: 82.7 us -> 81.5 us
    pallas_call x1, Pallas kernels: 82.7 us -> 81.5 us  [per_device(): pl.pallas_call(kernel, out_shape=(jax.ShapeDtypeStruct((N, W), F32), jax....]
where the time goes in v3:
time: 91.6 us; the launch traced here: 90.4 us
  Pallas kernels  81.5 us (89%)
  between operations  5.44 us (6%)
  local copies, waits for them, and re-layouts  3.55 us (4%)
    pallas_call x1, Pallas kernels, per_device(): pl.pallas_call(kernel, out_shape=(jax.ShapeDtypeStruct((N, W), F32), jax....  81.5 us
    unnamed x6, local copies, waits for them, and re-layouts  3.55 us

profile of v3, /device:TPU:32, one launch (start us, length us, event | category | flops | bytes accessed | tf_op | source)
XLA Modules:
  0.0 90.4 jit_solution(4782343279015974781)
XLA Ops:
  1.9 0.0 copy-start
  1.9 1.0 %copy-done = bf16[128,1152]{1,0:T(8,128)(2,1)S(1)} copy-done((bf16[128,1152]{1,0:T(8,128)(2,1)S(1)}, bf16[128,1152]{1,0:T(8,128)(2,1)}, u32[]{:S(2)}) %copy-start) | copy-done | bytes 294936
  2.9 0.0 copy-start.1
  2.9 1.0 %copy-done.1 = bf16[128,1152]{1,0:T(8,128)(2,1)S(1)} copy-done((bf16[128,1152]{1,0:T(8,128)(2,1)S(1)}, bf16[128,1152]{1,0:T(8,128)(2,1)}, u32[]{:S(2)}) %copy-start.1) | copy-done | bytes 294936
  3.8 81.5 %shard_map.75 = (f32[128,1152]{1,0:T(8,128)S(1)}, f32[128,1152]{1,0:T(8,128)S(1)}, f32[1]{0:T(128)}, f32[1]{0:T(128)}) custom-call(bf16[128,1152]{1,0:T(8,128)(2,1)S(1)} %copy-done, bf16[128,1152]{1,0:T(8,128)(2,1)S(1)} %copy-done.1, f32[1]{0:T(128)S(6)} %copy.12.log_temp, f32[1]{0:T(128)S(6)} %copy.13.bias), custom_call_target="tpu_custom_call" | custom-call | tf_op jit(solution)/shard_map/pallas_call | solution.py:550
  85.3 0.8 copy.14
  86.1 0.8 copy.15
Async XLA Ops:
  1.9 1.0 %copy-start = (bf16[128,1152]{1,0:T(8,128)(2,1)S(1)}, bf16[128,1152]{1,0:T(8,128)(2,1)}, u32[]{:S(2)}) copy-start(bf16[128,1152]{1,0:T(8,128)(2,1)} %images.1) | copy-start | bytes 884740
  2.9 1.0 %copy-start.1 = (bf16[128,1152]{1,0:T(8,128)(2,1)S(1)}, bf16[128,1152]{1,0:T(8,128)(2,1)}, u32[]{:S(2)}) copy-start(bf16[128,1152]{1,0:T(8,128)(2,1)} %texts.1) | copy-start | bytes 884740

commit v4 on v2

--- a/solution.py
+++ b/solution.py
@@ -167,13 +167,13 @@
         inverse = lax.rsqrt(jnp.sum(full * full, axis=-1, keepdims=True) + 1e-06)
         return full * inverse, inverse
 
-    tbuf[3, 0:N] = unit_rows(texts)[0].astype(BF16)
     ibuf[0, 0:N] = unit_rows(images)[0].astype(BF16)
     pl.semaphore_wait(barrier, len(peers))
-    start(right[0], left[0], swap[0], across[0][0])
+    start(swap[0], across[0][0])
     start_if(y > 0, direct[3][0])
     start_if(y == 3, direct[1][0])
-    start(right[1], left[1], swap[1], across[0][1])
+    tbuf[3, 0:N] = unit_rows(texts)[0].astype(BF16)
+    start(right[0], left[0], swap[1], across[0][1], right[1], left[1])
     start_if(y > 0, direct[3][1])
     start_if(y == 3, direct[1][1])
     start(twins[0])

time: 91.9 us -> 91.8 us (level)
  no operation moved by 1% of the time
where the time goes in v4:
time: 91.8 us; the launch traced here: 91.6 us
  Pallas kernels  82.6 us (90%)
  between operations  5.44 us (6%)
  local copies, waits for them, and re-layouts  3.55 us (4%)
    pallas_call x1, Pallas kernels, per_device(): pl.pallas_call(kernel, out_shape=(jax.ShapeDtypeStruct((N, W), F32), jax....  82.6 us
    unnamed x6, local copies, waits for them, and re-layouts  3.55 us

profile of v4, /device:TPU:32, one launch (start us, length us, event | category | flops | bytes accessed | tf_op | source)
XLA Modules:
  0.0 91.6 jit_solution(4206974635066271953)
XLA Ops:
  1.9 0.0 copy-start
  1.9 1.0 %copy-done = bf16[128,1152]{1,0:T(8,128)(2,1)S(1)} copy-done((bf16[128,1152]{1,0:T(8,128)(2,1)S(1)}, bf16[128,1152]{1,0:T(8,128)(2,1)}, u32[]{:S(2)}) %copy-start) | copy-done | bytes 294936
  2.9 0.0 copy-start.1
  2.9 1.0 %copy-done.1 = bf16[128,1152]{1,0:T(8,128)(2,1)S(1)} copy-done((bf16[128,1152]{1,0:T(8,128)(2,1)S(1)}, bf16[128,1152]{1,0:T(8,128)(2,1)}, u32[]{:S(2)}) %copy-start.1) | copy-done | bytes 294936
  3.8 82.6 %shard_map.75 = (f32[128,1152]{1,0:T(8,128)S(1)}, f32[128,1152]{1,0:T(8,128)S(1)}, f32[1]{0:T(128)}, f32[1]{0:T(128)}) custom-call(bf16[128,1152]{1,0:T(8,128)(2,1)S(1)} %copy-done, bf16[128,1152]{1,0:T(8,128)(2,1)S(1)} %copy-done.1, f32[1]{0:T(128)S(6)} %copy.12.log_temp, f32[1]{0:T(128)S(6)} %copy.13.bias), custom_call_target="tpu_custom_call" | custom-call | tf_op jit(solution)/shard_map/pallas_call | solution.py:547
  86.5 0.8 copy.14
  87.3 0.8 copy.15
Async XLA Ops:
  1.9 1.0 %copy-start = (bf16[128,1152]{1,0:T(8,128)(2,1)S(1)}, bf16[128,1152]{1,0:T(8,128)(2,1)}, u32[]{:S(2)}) copy-start(bf16[128,1152]{1,0:T(8,128)(2,1)} %images.1) | copy-start | bytes 884740
  2.9 1.0 %copy-start.1 = (bf16[128,1152]{1,0:T(8,128)(2,1)S(1)}, bf16[128,1152]{1,0:T(8,128)(2,1)}, u32[]{:S(2)}) copy-start(bf16[128,1152]{1,0:T(8,128)(2,1)} %texts.1) | copy-start | bytes 884740
